TPU v7x, 32 devices: a whole 2x2x4 slice. The times are simulated.
32 devices in a mesh: seq: 8 (over y, x, core), grp: 4 (over z).
Axes of the slice: x: 2, y: 2, z: 4, core: 2. Of those that a mesh axis runs over, the one named last changes fastest.
Arguments:
- inputs: bfloat16 [4, 8192, 384], P('grp', 'seq'), may hold values from -6 to 6
- segment: int32 [4, 8192], P('grp', 'seq'), may hold values from 0 to 3, never falling along the last dimension, each value on 1 to 4096 neighbouring positions
- conv_weight: bfloat16 [5, 384, 384], P(None, 'grp'), may hold values from -0.125 to 0.125
- proj_weight: bfloat16 [384, 448], P('grp'), may hold values from -0.3125 to 0.3125
- cotangent: bfloat16 [4, 4096, 448], P('grp', 'seq'), may hold values from -6 to 6
Outputs:
- pooled_out: bfloat16 [4, 4096, 448], P('grp', 'seq')
- input_grad: bfloat16 [4, 8192, 384], P('grp', 'seq')
- conv_grad: float32 [5, 384, 384], P(None, 'grp', 'seq')
- proj_grad: float32 [384, 448], P('grp', 'seq')
Inputs may be any that keep to these rules, and one draw needn't show every extreme that they name: `segment`: along each window the interval numbers never fall; every interval covers 1 to 4096 positions and one covers exactly 4096.
All inputs are finite; a program needn't handle non-finite values.
Results may differ from a plain program's by a relative error of at most 0.018.
Values may be sent and summed in bfloat16 or wider, within the bound.
A program may use at most 64 MiB of HBM per device.

v0:
```python
import math

import jax
import jax.numpy as jnp
from jax import lax
from jax.sharding import PartitionSpec as P


def extended(cells, sides, width):
    for axis, dim in sides:
        count = lax.axis_size(axis)
        ends = count - 1
        head = lax.slice_in_dim(cells, 0, width, axis=dim)
        tail = lax.slice_in_dim(cells, cells.shape[dim] - width, cells.shape[dim], axis=dim)
        cells = jnp.concatenate(
            [
                lax.ppermute(tail, axis, [(i, (i + 1) % count) for i in range(ends)]),
                cells,
                lax.ppermute(head, axis, [((i + 1) % count, i) for i in range(ends)]),
            ],
            axis=dim,
        )
    return cells


def gelu_slope(normed):
    cdf = 0.5 * (1.0 + jax.scipy.special.erf(normed / math.sqrt(2.0)))
    density = jnp.exp(-0.5 * normed * normed) / math.sqrt(2.0 * math.pi)
    return cdf + normed * density


def body(inputs, segment, conv_weight, proj_weight, cotangent):
    x_rows = inputs[0]
    seg_rows = segment[0]
    cot_rows = cotangent[0]
    length = x_rows.shape[0]
    wide = x_rows.astype(jnp.float32)
    inverse = lax.rsqrt(jnp.mean(wide * wide, axis=-1, keepdims=True) + 1e-06)
    normed = wide * inverse
    act = jax.nn.gelu(normed, approximate=False).astype(jnp.bfloat16)
    act_pad, seg_pad = (extended(act, (("seq", 0),), 2), extended(seg_rows, (("seq", 0),), 2))
    masks = [(seg_pad[j : j + length] == seg_rows)[:, None] for j in range(5)]
    zero_act = jnp.zeros((), jnp.bfloat16)
    shifted = jnp.stack([jnp.where(masks[j], act_pad[j : j + length], zero_act) for j in range(5)])
    conv_full, proj_full = (
        lax.all_gather(conv_weight, "grp", axis=1, tiled=True),
        lax.all_gather(proj_weight, "grp", axis=0, tiled=True),
    )
    conv_out = jnp.einsum("jrc,jcd->rd", shifted, conv_full, preferred_element_type=jnp.float32)
    hidden = (wide + conv_out).astype(jnp.bfloat16)
    paired = hidden.astype(jnp.float32).reshape(length // 2, 2, -1)
    pooled = ((paired[:, 0] + paired[:, 1]) * 0.5).astype(jnp.bfloat16)
    pooled_out = jnp.dot(pooled, proj_full, preferred_element_type=jnp.float32).astype(jnp.bfloat16)
    pool_grad = lax.dot_general(
        cot_rows, proj_full, (((1,), (1,)), ((), ())), preferred_element_type=jnp.float32
    )
    hidden_grad = jnp.repeat(pool_grad * 0.5, 2, axis=0).astype(jnp.bfloat16)
    proj_term = lax.dot_general(
        pooled, cot_rows, (((0,), (0,)), ((), ())), preferred_element_type=jnp.float32
    )
    conv_term = jnp.einsum("jrc,rd->jcd", shifted, hidden_grad, preferred_element_type=jnp.float32)
    grad_pad = extended(hidden_grad, (("seq", 0),), 2)
    zero_grad = jnp.zeros((), jnp.bfloat16)
    back_shift = jnp.stack(
        [jnp.where(masks[4 - k], grad_pad[4 - k : 4 - k + length], zero_grad) for k in range(5)]
    )
    act_grad = jnp.einsum("krd,kcd->rc", back_shift, conv_full, preferred_element_type=jnp.float32)
    norm_grad = act_grad * gelu_slope(normed)
    centred = norm_grad - normed * jnp.mean(norm_grad * normed, axis=-1, keepdims=True)
    input_grad = (hidden_grad.astype(jnp.float32) + centred * inverse).astype(jnp.bfloat16)
    conv_part, proj_part = (
        lax.psum_scatter(
            conv_term.astype(jnp.bfloat16), "grp", scatter_dimension=1, tiled=True
        ).astype(jnp.float32),
        lax.psum_scatter(
            proj_term.astype(jnp.bfloat16), "grp", scatter_dimension=0, tiled=True
        ).astype(jnp.float32),
    )
    conv_grad, proj_grad = (
        lax.psum_scatter(
            conv_part.astype(jnp.bfloat16), "seq", scatter_dimension=2, tiled=True
        ).astype(jnp.float32),
        lax.psum_scatter(
            proj_part.astype(jnp.bfloat16), "seq", scatter_dimension=1, tiled=True
        ).astype(jnp.float32),
    )
    return (pooled_out[None], input_grad[None], conv_grad, proj_grad)


def solution(mesh):
    return jax.shard_map(
        body,
        mesh=mesh,
        in_specs=(
            P("grp", "seq", None),
            P("grp", "seq"),
            P(None, "grp", None),
            P("grp", None),
            P("grp", "seq", None),
        ),
        out_specs=(
            P("grp", "seq", None),
            P("grp", "seq", None),
            P(None, "grp", "seq"),
            P("grp", "seq"),
        ),
        check_vma=False,
    )
```

profile of v0, /device:TPU:0, one launch (start us, length us, event | category | flops | bytes accessed | tf_op | source)
XLA Modules:
  0.0 250.8 jit_solution(18396676666582661644)
XLA Ops:
  7.2 16.6 %all_gather.7 = bf16[384,448]{1,0:T(8,128)(2,1)S(1)} all-gather(bf16[96,448]{1,0:T(8,128)(2,1)} %param.8), channel_id=1, replica_groups=mesh['seq'=8,'grp'=4] {'grp'}, dimensions={0}, use_global_device_ids=true | all-gather | bytes 430080 | tf_op jit(solution)/shard_map/all_gather | solution.py:47
  23.8 0.5 fusion.84
  24.4 1.3 collective-permute-start.4
  25.7 0.1 slice_bitcast_fusion
  25.8 3.0 %collective-permute-start = (s32[2]{0:T(128)S(1)}, s32[2]{0:T(128)S(1)}, u32[]{:S(2)}, u32[]{:S(2)}) collective-permute-start(s32[2]{0:T(128)S(1)} %get-tuple-element.31), channel_id=1, source_target_pairs={{0,4},{4,8},{8,12},{12,16},{16,20},{20,24},{24,28},{1,5},{5,9},{9,... | collective-permute-start | bytes 32 | tf_op jit(solution)/shard_map/ppermute | solution.py:17
  28.8 1.3 collective-permute-start.2
  30.1 3.6 %collective-permute-start.5 = (bf16[2,384]{1,0:T(2,128)(2,1)S(1)}, bf16[2,384]{1,0:T(2,128)(2,1)S(1)}, u32[]{:S(2)}, u32[]{:S(2)}) collective-permute-start(bf16[2,384]{1,0:T(2,128)(2,1)S(1)} %slice.113), channel_id=1, source_target_pairs={{0,4},{4,8},{8,12},{12,16},{16,20},{20,24},{24,28},{1,5},{5,9},{9,... | collective-permute-start | bytes 4616 | tf_op jit(solution)/shard_map/ppermute | solution.py:17
  33.8 0.4 broadcast_in_dim.76
  34.2 0.3 convert_element_type.79
  34.5 1.2 convert_element_type.81
  35.7 0.1 constant_dynamic-update-slice_fusion.1
  35.8 0.2 fusion.79
  36.1 0.1 fusion.122
  36.2 1.2 fusion.106
  37.3 1.2 fusion.104
  38.6 0.9 constant_dynamic-update-slice_fusion.2
  39.5 1.2 fusion.90
  40.7 1.2 fusion.102
  41.9 21.9 %all-gather.2.cloned.1.call-done = bf16[5,384,384]{2,1,0:T(8,128)(2,1)} async-done(((bf16[5,96,384]{2,1,0:T(8,128)(2,1)}), bf16[5,384,384]{2,1,0:T(8,128)(2,1)}) %all-gather.2.cloned.1.call-update) | async-done | bytes 1474576 | tf_op jit(solution)/shard_map/all_gather | solution.py:46
  63.8 5.2 %fusion.78 = (f32[1024]{0:T(1024)S(1)}, f32[1024,384]{1,0:T(8,128)S(1)}) fusion(bf16[1,1024,384]{2,1,0:T(8,128)(2,1)S(1)} %copy-done.1, f32[1024]{0:T(1024)S(1)} %add_rsqrt_fusion, bf16[5,1024,384]{2,1,0:T(8,128)(2,1)} %fusion.102, bf16[5,384,384]{2,1,0:T(8,128)(2,1)} %all-gather.2.cloned.1.call-done), kind=kOutput, calls=%fused_computation.84 | convolution fusion | flops 1515060224 | bytes 7774208 | tf_op jit(solution)/shard_map/krd,kcd->rc/dot_general | solution.py:67
  69.1 5.1 %fusion.99 = (bf16[1,1024,384]{2,1,0:T(8,128)(2,1)}, bf16[1024,384]{1,0:T(8,128)(2,1)S(1)}) fusion(f32[1024,384]{1,0:T(8,128)S(1)} %get-tuple-element.33, bf16[1,1024,384]{2,1,0:T(8,128)(2,1)S(1)} %copy-done.1, bf16[1024,384]{1,0:T(8,128)(2,1)S(1)} %convert_element_type.79, f32[1024]{0:T(1024)S(1)} %broadcast_multiply_fusion, f32[1024]{0:T(1024)S(1)} %add_rsqrt_fusion), kind=kLoop, calls=%fused_computation.114 | loop fusion | flops 28704768 | bytes 4726784 | tf_op jit(solution)/shard_map/broadcast_in_dim | solution.py:87
  74.2 1.3 collective-permute-start.1
  75.5 1.5 collective-permute-start.3
  77.0 0.3 fusion.98
  77.3 0.4 fusion.112
  77.6 4.7 %fusion.86 = bf16[5,1024,384]{2,1,0:T(8,128)(2,1)S(1)} fusion(bf16[5,1024,384]{2,1,0:T(8,128)(2,1)S(1)} %fusion.112, bf16[1,1024,384]{2,1,0:T(8,128)(2,1)S(1)} %copy-done.1, f32[1024]{0:T(1024)S(1)} %add_rsqrt_fusion), kind=kLoop, calls=%fused_computation.101 | loop fusion | flops 26345472 | bytes 1576960
  82.4 0.4 fusion.94
  82.8 0.4 fusion.109
  83.2 1.9 copy-done.3
  85.1 3.4 %fusion.83 = f32[1024,384]{1,0:T(8,128)} fusion(bf16[5,1024,384]{2,1,0:T(8,128)(2,1)S(1)} %fusion.109, bf16[5,384,384]{2,1,0:T(8,128)(2,1)S(1)} %copy-done.5, bf16[1,1024,384]{2,1,0:T(8,128)(2,1)S(1)} %copy-done.1), kind=kOutput, calls=%fused_computation.89 | convolution fusion | flops 1511522304 | bytes 7766016 | tf_op jit(solution)/shard_map/jrc,jcd->rd/dot_general | solution.py:49
  88.5 2.2 reshape.73
  90.7 1.2 fusion.124
  91.9 0.1 fusion.117
  92.1 1.2 convolution_convert_fusion.2
  93.3 0.0 reduce-scatter.5.cloned.1.call-start
  93.3 0.3 reshape.76
  93.6 5.5 %convolution_convert_fusion = bf16[5,384,384]{2,1,0:T(8,128)(2,1)} fusion(bf16[5,1024,384]{2,1,0:T(8,128)(2,1)} %copy-done.3, bf16[1024,384,1]{1,0,2:T(8,128)(2,1)S(1)} %reshape.76), kind=kOutput, calls=%fused_computation.16 | convolution fusion | flops 1510686720 | bytes 6193152 | tf_op jit(solution)/shard_map/jrc,rd->jcd/dot_general | solution.py:61
  99.1 0.0 all-reduce.3.cloned.1.call-start
  99.1 16.7 %reduce-scatter.9.cloned.1.call-done = bf16[96,448]{1,0:T(8,128)(2,1)} async-done(((bf16[384,448]{1,0:T(8,128)(2,1)}), bf16[96,448]{1,0:T(8,128)(2,1)}) %reduce-scatter.9.cloned.1.call-update) | async-done | bytes 86032 | tf_op jit(solution)/shard_map/reduce_scatter | solution.py:75
  115.9 34.5 %reduce-scatter.5.cloned.1.call-done = bf16[5,96,384]{2,1,0:T(8,128)(2,1)} async-done(((bf16[5,384,384]{2,1,0:T(8,128)(2,1)}), bf16[5,96,384]{2,1,0:T(8,128)(2,1)}) %reduce-scatter.5.cloned.1.call-update) | async-done | bytes 368656 | tf_op jit(solution)/shard_map/reduce_scatter | solution.py:72
  150.4 2.3 copy.23
  152.7 0.6 dynamic-slice
  154.0 1.2 fusion.85
  155.2 48.5 %all-reduce.3.cloned.1.call-done = bf16[96,448]{1,0:T(8,128)(2,1)} async-done(((bf16[96,448]{1,0:T(8,128)(2,1)}), bf16[96,448]{1,0:T(8,128)(2,1)}) %all-reduce.3.cloned.1.call-update) | async-done | bytes 86032
  203.7 0.9 dynamic-slice_convert_fusion
  204.5 0.7 copy.25
  205.2 37.5 %reduce-scatter.7.cloned.1.call-done = bf16[5,96,48]{1,0,2:T(8,128)(2,1)} async-done(((bf16[5,96,384]{1,0,2:T(8,128)(2,1)}), bf16[5,96,48]{1,0,2:T(8,128)(2,1)}) %reduce-scatter.7.cloned.1.call-update) | async-done | bytes 46096 | tf_op jit(solution)/shard_map/reduce_scatter | solution.py:80
  242.8 1.5 copy.24
  (34 shorter events, 0.3 us)
Async XLA Ops:
  7.2 16.7 %copy-start = (bf16[1,512,448]{1,2,0:T(8,128)(2,1)S(1)}, bf16[1,512,448]{1,2,0:T(8,128)(2,1)}, u32[]{:S(2)}) copy-start(bf16[1,512,448]{1,2,0:T(8,128)(2,1)} %param.9) | copy-start | bytes 1376260
  7.2 18.5 %copy-start.4 = (s32[1,1024]{1,0:T(1,128)S(1)}, s32[1,1024]{1,0:T(1,128)}, u32[]{:S(2)}) copy-start(s32[1,1024]{1,0:T(1,128)} %param.6) | copy-start | bytes 12292
  7.2 56.6 %all-gather.2.cloned.1.call-start = ((), (), s32[]{:S(2)}) async-start(), calls=%async_computation.3 | async-start | bytes 1843200 | tf_op jit(solution)/shard_map/all_gather | solution.py:46
  24.4 11.8 %collective-permute-start.4 = (bf16[2,384]{1,0:T(2,128)(2,1)S(1)}, bf16[2,384]{1,0:T(2,128)(2,1)S(1)}, u32[]{:S(2)}, u32[]{:S(2)}) collective-permute-start(bf16[2,384]{1,0:T(2,128)(2,1)S(1)} %slice.108), channel_id=1, source_target_pairs={{4,0},{8,4},{12,8},{16,12},{20,16},{24,20},{28,24},{5,1},{9,5},{13... | collective-permute-start | bytes 4616 | tf_op jit(solution)/shard_map/ppermute | solution.py:19
  25.7 90.1 %reduce-scatter.9.cloned.1.call-start = ((), (), s32[]{:S(2)}) async-start(), calls=%async_computation.6 | async-start | bytes 491520 | tf_op jit(solution)/shard_map/reduce_scatter | solution.py:75
  25.8 10.2 %collective-permute-start = (s32[2]{0:T(128)S(1)}, s32[2]{0:T(128)S(1)}, u32[]{:S(2)}, u32[]{:S(2)}) collective-permute-start(s32[2]{0:T(128)S(1)} %get-tuple-element.31), channel_id=1, source_target_pairs={{0,4},{4,8},{8,12},{12,16},{16,20},{20,24},{24,28},{1,5},{5,9},{9,... | collective-permute-start | bytes 32 | tf_op jit(solution)/shard_map/ppermute | solution.py:17
  28.8 7.2 %collective-permute-start.2 = (s32[2]{0:T(128)S(1)}, s32[2]{0:T(128)S(1)}, u32[]{:S(2)}, u32[]{:S(2)}) collective-permute-start(s32[2]{0:T(128)S(1)} %get-tuple-element.30), channel_id=1, source_target_pairs={{4,0},{8,4},{12,8},{16,12},{20,16},{24,20},{28,24},{5,1},{9,5},{13... | collective-permute-start | bytes 32 | tf_op jit(solution)/shard_map/ppermute | solution.py:19
  30.1 9.4 %collective-permute-start.5 = (bf16[2,384]{1,0:T(2,128)(2,1)S(1)}, bf16[2,384]{1,0:T(2,128)(2,1)S(1)}, u32[]{:S(2)}, u32[]{:S(2)}) collective-permute-start(bf16[2,384]{1,0:T(2,128)(2,1)S(1)} %slice.113), channel_id=1, source_target_pairs={{0,4},{4,8},{8,12},{12,16},{16,20},{20,24},{24,28},{1,5},{5,9},{9,... | collective-permute-start | bytes 4616 | tf_op jit(solution)/shard_map/ppermute | solution.py:17
  34.5 1.3 copy-start.1
  36.2 2.4 copy-start.2
  74.2 2.8 %collective-permute-start.1 = (bf16[2,384]{1,0:T(2,128)(2,1)S(1)}, bf16[2,384]{1,0:T(2,128)(2,1)S(1)}, u32[]{:S(2)}, u32[]{:S(2)}) collective-permute-start(bf16[2,384]{1,0:T(2,128)(2,1)S(1)} %get-tuple-element.23), channel_id=1, source_target_pairs={{0,4},{4,8},{8,12},{12,16},{16,20},{20,24},{24,28},{1,5},{5,9},{9,... | collective-permute-start | bytes 4616 | tf_op jit(solution)/shard_map/ppermute | solution.py:17
  75.5 6.9 %collective-permute-start.3 = (bf16[2,384]{1,0:T(2,128)(2,1)S(1)}, bf16[2,384]{1,0:T(2,128)(2,1)S(1)}, u32[]{:S(2)}, u32[]{:S(2)}) collective-permute-start(bf16[2,384]{1,0:T(2,128)(2,1)S(1)} %get-tuple-element.22), channel_id=1, source_target_pairs={{4,0},{8,4},{12,8},{16,12},{20,16},{24,20},{28,24},{5,1},{9,5},{13... | collective-permute-start | bytes 4616 | tf_op jit(solution)/shard_map/ppermute | solution.py:19
  82.4 2.7 %copy-start.5 = (bf16[5,384,384]{2,1,0:T(8,128)(2,1)S(1)}, bf16[5,384,384]{2,1,0:T(8,128)(2,1)}, u32[]{:S(2)}) copy-start(bf16[5,384,384]{2,1,0:T(8,128)(2,1)} %all-gather.2.cloned.1.call-done) | copy-start | bytes 4423684
  83.2 1.9 copy-start.3
  93.3 57.1 %reduce-scatter.5.cloned.1.call-start = ((), (), s32[]{:S(2)}) async-start(), calls=%async_computation.4 | async-start | bytes 1843200 | tf_op jit(solution)/shard_map/reduce_scatter | solution.py:72
  99.1 53.6 %copy-start.6 = (u32[32]{0:T(128)S(1)}, u32[32]{0:T(128)}, u32[]{:S(2)}) copy-start(u32[32]{0:T(128)} %constant.83) | copy-start | bytes 388
  99.1 104.6 %all-reduce.3.cloned.1.call-start = ((), (), s32[]{:S(2)}) async-start(), calls=%async_computation.7 | async-start | bytes 196608
  115.8 126.9 %reduce-scatter.7.cloned.1.call-start = ((), (), s32[]{:S(2)}) async-start(), calls=%async_computation.5 | async-start | bytes 884736 | tf_op jit(solution)/shard_map/reduce_scatter | solution.py:80
Sparse Core Ops, SparseCore 0:
  25.8 37.9 all-gather.1
  93.4 22.3 reduce-scatter.8
  118.3 32.0 reduce-scatter.4
  153.3 50.3 all-reduce.2
  207.0 35.7 reduce-scatter.6
where the time goes:
time: 251 us
  waiting for transfers between devices  159 us (63%)
  other arithmetic  17.4 us (7%)
  matrix products  17 us (7%)
  blocking collectives  16.6 us (7%)
  between operations  14.7 us (6%)
  local copies, waits for them, and re-layouts  13.8 us (5%)
  starting transfers between devices  12.2 us (5%)
    unnamed x6, waiting for transfers between devices  48.6 us
    reduce_scatter x1, waiting for transfers between devices, body(): lax.psum_scatter(conv_part.astype(jnp.bfloat16), 'seq', scatter_dimension...  37.5 us
    reduce_scatter x1, waiting for transfers between devices, body(): lax.psum_scatter(conv_term.astype(jnp.bfloat16), 'grp', scatter_dimension...  34.5 us
    all_gather x1, waiting for transfers between devices, body(): lax.all_gather(conv_weight, 'grp', axis=1, tiled=True)  21.9 us
    reduce_scatter x1, waiting for transfers between devices, body(): lax.psum_scatter(proj_term.astype(jnp.bfloat16), 'grp', scatter_dimension...  16.7 us
    all_gather x1, blocking collectives, body(): lax.all_gather(proj_weight, 'grp', axis=0, tiled=True)  16.6 us
    unnamed x7, other arithmetic  9.39 us
    ppermute x3, starting transfers between devices, extended(): lax.ppermute(tail, axis, [(i, (i + 1) % count) for i in range(ends)])  7.94 us
  transfers between devices with their start and end apart: 11, of which 5 were waited for; matrix products, arithmetic and copies ran while one was open for 10% of the time, Pallas kernels for 0%

commit v1 on v0

v1 whole, which is shorter than its diff:
```python
import functools
import math

import jax
import jax.numpy as jnp
from jax import lax
from jax.experimental import pallas as pl
from jax.experimental.pallas import tpu as pltpu
from jax.sharding import PartitionSpec as P

F32 = jnp.float32
BF16 = jnp.bfloat16
TAPS = 5
EDGE = 16
NT = (((1,), (1,)), ((), ()))


def up16(n):
    return -(-n // 16) * 16


def dot(a, b, dims=(((1,), (0,)), ((), ()))):
    return lax.dot_general(a, b, dims, preferred_element_type=F32)


def normalised(x):
    inverse = lax.rsqrt(jnp.mean(x * x, axis=-1, keepdims=True) + 1e-06)
    return x * inverse, inverse


def gate(r):
    return 0.5 * (1.0 + lax.erf(r * (1.0 / math.sqrt(2.0))))


def pick(rows, cols, first, per):
    r = lax.broadcasted_iota(jnp.int32, (rows, cols), 0)
    c = lax.broadcasted_iota(jnp.int32, (rows, cols), 1)
    return jnp.where(r // per + first == c, 1.0, 0.0)


class Sizes:
    def __init__(self, mesh, x, conv, proj, cot):
        self.n_seq, self.n_grp = mesh.shape["seq"], mesh.shape["grp"]
        self.n_chip = self.n_seq // 2
        self.rows, self.c0 = x
        self.half, self.c1 = cot
        self.cs = conv[1]
        self.gpt = -(-self.cs // 16)
        self.gpp = -(-TAPS * self.gpt // self.n_seq)
        self.ppp = -(-self.gpt // self.n_seq)
        self.dc, self.dp = self.c0 // self.n_seq, self.c1 // self.n_seq
        self.rc, self.rp = up16(self.dc), up16(self.dp)
        self.stage = BF16 if self.cs % 16 == 0 else F32


def scratch(z):
    ext = z.rows + 2 * EDGE
    V, S = pltpu.VMEM, pltpu.SemaphoreType.DMA
    shapes = dict(
        xh=V((2, EDGE, z.c0), BF16),
        ch=V((2, EDGE, z.c1), BF16),
        sh=V((2, EDGE, 128), jnp.int32),
        seg=V((ext, 128), jnp.int32),
        act=V((ext, z.c0), F32),
        slope=V((z.rows, z.c0), F32),
        grad=V((ext, z.c0), F32),
        gradt=V((z.c0, z.rows), BF16),
        shifted=V((z.rows, TAPS * z.c0), BF16),
        pooled=V((z.half, z.c0), BF16),
        wbuf=V((z.n_grp, z.n_chip, 2, 16 * z.gpp, z.c0), BF16),
        pbuf=V((z.n_grp, z.n_chip, 2, 16 * z.ppp, z.c1), BF16),
        wf=V((TAPS * z.c0, z.c0), z.stage),
        wb=V((z.c0, TAPS * z.c0), z.stage),
        pf=V((z.c0, z.c1), z.stage),
        halo_s=S((6,)),
        halo_r=S((6,)),
        gc_s=S((2, z.n_grp)),
        gc_r=S((2, z.n_grp)),
        gb_s=S((2, z.n_chip)),
        gb_r=S((2, z.n_chip)),
        ga_s=S((2,)),
        ga_r=S((2,)),
        ra_s=S((TAPS + 1,)),
        ra_r=S((TAPS + 1,)),
        rb_s=S((TAPS + 1, z.n_chip)),
        rb_r=S((TAPS + 1, z.n_chip)),
        rc_s=S((TAPS + 1, z.n_grp)),
        rc_r=S((TAPS + 1, z.n_grp)),
    )
    for name, units, r in (("c", TAPS, z.rc), ("p", 1, z.rp)):
        lanes = z.c0 // z.n_grp
        shapes.update({
            name + "_acc": V((units, z.n_chip, 2, r, z.c0), F32),
            name + "_sa": V((units, z.n_chip, r, z.c0), BF16),
            name + "_ra": V((units, z.n_chip, r, z.c0), BF16),
            name + "_kb": V((units, z.n_chip, r, z.c0), F32),
            name + "_sb": V((units, z.n_chip, r, z.c0), BF16),
            name + "_rb": V((units, z.n_chip, r, z.c0), BF16),
            name + "_kc": V((units, z.n_grp, r, lanes), F32),
            name + "_sc": V((units, z.n_grp, r, lanes), BF16),
            name + "_rc": V((units, z.n_grp, r, lanes), BF16),
        })
    return shapes


def kernel(z, names, x_ref, seg_ref, conv_ref, proj_ref, cot_ref, po_ref, ig_ref, cg_ref, pg_ref, *refs):
    m = dict(zip(names, refs))
    s, g = lax.axis_index("seq"), lax.axis_index("grp")
    chip, core = s // 2, s % 2
    sent = []

    def at(s2, g2):
        return {"seq": s2, "grp": g2}

    def turn(i, k, n):
        return lax.rem(i + k, n)

    def remote(src, dst, ss, rs, to):
        return pltpu.make_async_remote_copy(
            src_ref=src, dst_ref=dst, send_sem=ss, recv_sem=rs, device_id=to, device_id_type=pl.DeviceIdType.MESH
        )

    def go(copies):
        for c in copies:
            c.start()
        sent.extend(copies)

    def landed(copies):
        for c in copies:
            c.wait_recv()

    left, right = turn(s, z.n_seq - 1, z.n_seq), turn(s, 1, z.n_seq)
    sibling = chip * 2 + (1 - core)
    across = turn(s, z.n_seq - 1 + 2 * core, z.n_seq)

    def chip_peer(k):
        return at(turn(chip, k, z.n_chip) * 2 + core, g)

    def grp_peer(k):
        return at(s, turn(g, k, z.n_grp))

    barrier = pltpu.get_barrier_semaphore()
    peers = [at(sibling, g), at(across, g)]
    peers += [chip_peer(k) for k in range(1, z.n_chip)] + [grp_peer(k) for k in range(1, z.n_grp)]
    for to in peers:
        pl.semaphore_signal(barrier, inc=1, device_id=to, device_id_type=pl.DeviceIdType.MESH)

    for q in range(TAPS * z.gpt):
        j, r = q // z.gpt, (q % z.gpt) * 16
        h = min(16, z.cs - r)
        piece, o = q // z.gpp, (q % z.gpp) * 16
        m["wbuf"][0, piece // 2, piece % 2, o : o + h, :] = conv_ref[j, r : r + h, :]
    for q in range(z.gpt):
        r = q * 16
        h = min(16, z.cs - r)
        piece, o = q // z.ppp, (q % z.ppp) * 16
        m["pbuf"][0, piece // 2, piece % 2, o : o + h, :] = proj_ref[r : r + h, :]
    m["seg"][EDGE : EDGE + z.rows, :] = jnp.broadcast_to(seg_ref[...], (128, z.rows)).T

    pl.semaphore_wait(barrier, len(peers))

    def gather_c(i, buf):
        return [
            remote(buf.at[0, chip, core], buf.at[k, chip, core], m["gc_s"].at[i, k], m["gc_r"].at[i, k], grp_peer(k))
            for k in range(1, z.n_grp)
        ]

    def gather_b(i, buf):
        part = buf.at[pl.ds(1, z.n_grp - 1), chip, core]
        return [
            remote(part, part, m["gb_s"].at[i, k], m["gb_r"].at[i, k], chip_peer(k)) for k in range(1, z.n_chip)
        ]

    def gather_a(i, buf):
        part = buf.at[pl.ds(1, z.n_grp - 1), :, core]
        return [remote(part, part, m["ga_s"].at[i], m["ga_r"].at[i], at(sibling, g))]

    go(pc := gather_c(0, m["pbuf"]))
    halos = []
    ends = (pl.ds(0, EDGE), pl.ds(z.rows - EDGE, EDGE))
    cot_ends = (pl.ds(0, EDGE), pl.ds(z.half - EDGE, EDGE))
    seg_ends = (pl.ds(EDGE, EDGE), pl.ds(z.rows, EDGE))
    for i, (src, dst, cuts) in enumerate(
        ((x_ref, m["xh"], ends), (cot_ref, m["ch"], cot_ends), (m["seg"], m["sh"], seg_ends))
    ):
        for side, to in ((1, left), (0, right)):
            halos.append(remote(
                src.at[cuts[1 - side]], dst.at[side], m["halo_s"].at[2 * i + side], m["halo_r"].at[2 * i + side], at(to, g)
            ))
    go(halos)
    go(wc := gather_c(1, m["wbuf"]))

    def act_rows(first, count):
        def step(t, _):
            b = pl.multiple_of(t * 32, 32)
            r, _inv = normalised(x_ref[pl.ds(b, 32), :].astype(F32))
            cdf = gate(r)
            m["act"][pl.ds(EDGE + b, 32), :] = (r * cdf).astype(BF16).astype(F32)
            m["slope"][pl.ds(b, 32), :] = cdf + r * (jnp.exp(-0.5 * r * r) * (1.0 / math.sqrt(2.0 * math.pi)))
            return 0

        lax.fori_loop(first // 32, (first + count) // 32, step, 0)

    act_rows(0, z.rows // 2)
    landed(pc)
    go(pb := gather_b(0, m["pbuf"]))
    act_rows(z.rows // 2, z.rows // 2)
    landed(wc)
    go(wb := gather_b(1, m["wbuf"]))

    landed(halos)
    for side, where in ((0, 0), (1, EDGE + z.rows)):
        r, _inv = normalised(m["xh"][side].astype(F32))
        m["act"][where : where + EDGE, :] = (r * gate(r)).astype(BF16).astype(F32)
        outside = (s == 0) if side == 0 else (s == z.n_seq - 1)
        m["seg"][where : where + EDGE, :] = jnp.where(outside, -1, m["sh"][side])

    landed(pb)
    go(pa := gather_a(0, m["pbuf"]))

    def spread(src):
        def step(t, _):
            b = pl.multiple_of(t * 64, 64)
            seg = m["seg"][pl.ds(b, 64 + 2 * EDGE), :]
            own = seg[EDGE : EDGE + 64]
            masks = [seg[14 + j : 78 + j] == own for j in range(TAPS)]
            for o in range(0, z.c0, 128):
                window = src[pl.ds(b, 64 + 2 * EDGE), o : o + 128]
                for j in range(TAPS):
                    cut = jnp.where(masks[j], window[14 + j : 78 + j], 0.0).astype(BF16)
                    m["shifted"][pl.ds(b, 64), j * z.c0 + o : j * z.c0 + o + 128] = cut
            return 0

        lax.fori_loop(0, z.rows // 64, step, 0)

    spread(m["act"])

    landed(pa)
    for k in range(z.n_grp):
        base = lax.rem(g + z.n_grp - k, z.n_grp) * z.cs
        for q in range(z.gpt):
            r = q * 16
            h = min(16, z.cs - r)
            piece, o = q // z.ppp, (q % z.ppp) * 16
            rows = m["pbuf"][k, piece // 2, piece % 2, o : o + h, :].astype(z.stage)
            m["pf"][pl.ds(pl.multiple_of(base + r, math.gcd(z.cs, 16)), h), :] = rows
    proj = m["pf"][...].astype(BF16)

    pool_grad = (dot(cot_ref[...], proj, NT) * 0.5).astype(BF16)
    double = pick(256, 128, 0, 2).astype(BF16)
    for t in range(z.half // 128):
        hg = dot(double, pool_grad[t * 128 : t * 128 + 128])
        m["grad"][EDGE + t * 256 : EDGE + t * 256 + 256, :] = hg
        m["gradt"][:, t * 256 : t * 256 + 256] = hg.T.astype(BF16)
    for side, where in ((0, 0), (1, EDGE + z.rows)):
        pg = (dot(m["ch"][side], proj, NT) * 0.5).astype(BF16)
        chosen = pick(EDGE, EDGE, EDGE // 2 if side == 0 else 0, 2).astype(BF16)
        m["grad"][where : where + EDGE, :] = dot(chosen, pg)

    landed(wb)
    go(wa := gather_a(1, m["wbuf"]))

    def unit(u):
        return ("c", u, z.dc) if u < TAPS else ("p", 0, z.dp)

    live = {}

    def reduce_a(u, term):
        n, i, d = unit(u)
        acc = m[n + "_acc"]
        for b in range(z.n_seq):
            acc[i, b // 2, b % 2, 0:d, :] = term[b * d : b * d + d]
        for q in range(z.n_chip):
            m[n + "_sa"][i, q] = acc[i, q, 1 - core].astype(BF16)
        go(c := [remote(m[n + "_sa"].at[i], m[n + "_ra"].at[i], m["ra_s"].at[u], m["ra_r"].at[u], at(sibling, g))])
        live["a", u] = c

    def reduce_b(u):
        n, i, d = unit(u)
        landed(live["a", u])
        for q in range(z.n_chip):
            m[n + "_kb"][i, q] = m[n + "_acc"][i, q, core] + m[n + "_ra"][i, q].astype(F32)
        copies = []
        for k in range(1, z.n_chip):
            m[n + "_sb"][i, k] = m[n + "_kb"][i, turn(chip, k, z.n_chip)].astype(BF16)
            copies.append(remote(
                m[n + "_sb"].at[i, k], m[n + "_rb"].at[i, k], m["rb_s"].at[u, k], m["rb_r"].at[u, k], chip_peer(k)
            ))
        go(copies)
        live["b", u] = copies

    def reduce_c(u):
        n, i, d = unit(u)
        landed(live["b", u])
        total = m[n + "_kb"][i, chip]
        for k in range(1, z.n_chip):
            total = total + m[n + "_rb"][i, k].astype(F32)
        lanes = z.c0 // z.n_grp
        for k in range(z.n_grp):
            m[n + "_kc"][i, k] = total[:, k * lanes : k * lanes + lanes]
        copies = []
        for k in range(1, z.n_grp):
            m[n + "_sc"][i, k] = m[n + "_kc"][i, turn(g, k, z.n_grp)].astype(BF16)
            copies.append(remote(
                m[n + "_sc"].at[i, k], m[n + "_rc"].at[i, k], m["rc_s"].at[u, k], m["rc_r"].at[u, k], grp_peer(k)
            ))
        go(copies)
        live["c", u] = copies

    def reduce_end(u):
        n, i, d = unit(u)
        landed(live["c", u])
        total = m[n + "_kc"][i, g]
        for k in range(1, z.n_grp):
            total = total + m[n + "_rc"][i, k].astype(F32)
        if u < TAPS:
            cg_ref[u] = total[0:d]
        else:
            pg_ref[...] = total[0:d]

    for j in range(TAPS):
        reduce_a(j, dot(m["gradt"][...], m["shifted"][:, j * z.c0 : j * z.c0 + z.c0]))
        if j >= 1:
            reduce_b(j - 1)
        if j >= 3:
            reduce_c(j - 3)

    landed(wa)
    for k in range(z.n_grp):
        base = lax.rem(g + z.n_grp - k, z.n_grp) * z.cs
        for q in range(TAPS * z.gpt):
            j, r = q // z.gpt, (q % z.gpt) * 16
            h = min(16, z.cs - r)
            piece, o = q // z.gpp, (q % z.gpp) * 16
            rows = m["wbuf"][k, piece // 2, piece % 2, o : o + h, :].astype(z.stage)
            place = pl.multiple_of(base + r, math.gcd(z.cs, 16))
            m["wf"][pl.ds(j * z.c0 + place, h), :] = rows
            m["wb"][pl.ds(place, h), (TAPS - 1 - j) * z.c0 : (TAPS - j) * z.c0] = rows
    reduce_b(TAPS - 1)
    reduce_c(2)

    halve = (pick(256, 128, 0, 2).T * 0.5).astype(BF16)
    for t in range(z.rows // 256):
        a = t * 256
        conv = dot(m["shifted"][a : a + 256, :], m["wf"][...].astype(BF16))
        hidden = (x_ref[a : a + 256, :].astype(F32) + conv).astype(BF16)
        m["pooled"][a // 2 : a // 2 + 128, :] = dot(halve, hidden).astype(BF16)
    reduce_c(3)
    pooled = m["pooled"][...]
    reduce_a(TAPS, dot(cot_ref[...].T, pooled))
    po_ref[...] = dot(pooled, proj).astype(BF16)
    reduce_c(4)

    spread(m["grad"])
    reduce_b(TAPS)
    for t in range(z.rows // 256):
        a = t * 256
        act_grad = dot(m["shifted"][a : a + 256, :], m["wb"][...].astype(BF16), NT)
        m["act"][a : a + 256, :] = act_grad * m["slope"][a : a + 256, :]
        if t == 1:
            reduce_c(TAPS)

    def last(t, _):
        b = pl.multiple_of(t * 32, 32)
        r, inverse = normalised(x_ref[pl.ds(b, 32), :].astype(F32))
        ng = m["act"][pl.ds(b, 32), :]
        centred = ng - r * jnp.mean(ng * r, axis=-1, keepdims=True)
        ig_ref[pl.ds(b, 32), :] = (m["grad"][pl.ds(EDGE + b, 32), :] + centred * inverse).astype(BF16)
        return 0

    lax.fori_loop(0, z.rows // 32, last, 0)
    for u in range(TAPS + 1):
        reduce_end(u)
    for c in sent:
        c.wait_send()


def body(mesh, inputs, segment, conv_weight, proj_weight, cotangent):
    z = Sizes(mesh, inputs.shape[1:], conv_weight.shape, proj_weight.shape, cotangent.shape[1:])
    shapes = scratch(z)
    vmem = pl.BlockSpec(memory_space=pltpu.VMEM)
    lanes = z.c0 // z.n_grp
    po, ig, cg, pg = pl.pallas_call(
        functools.partial(kernel, z, tuple(shapes)),
        out_shape=(
            jax.ShapeDtypeStruct((z.half, z.c1), BF16),
            jax.ShapeDtypeStruct((z.rows, z.c0), BF16),
            jax.ShapeDtypeStruct((TAPS, z.dc, lanes), F32),
            jax.ShapeDtypeStruct((z.dp, lanes), F32),
        ),
        in_specs=[vmem] * 5,
        out_specs=[vmem] * 4,
        scratch_shapes=list(shapes.values()),
        compiler_params=pltpu.CompilerParams(
            collective_id=0, has_side_effects=True, vmem_limit_bytes=56 * 1024 * 1024
        ),
    )(inputs[0], segment, conv_weight, proj_weight, cotangent[0])
    return po[None], ig[None], jnp.swapaxes(cg, 1, 2), pg.T


def solution(mesh):
    return jax.shard_map(
        functools.partial(body, mesh),
        mesh=mesh,
        in_specs=(
            P("grp", "seq", None),
            P("grp", "seq"),
            P(None, "grp", None),
            P("grp", None),
            P("grp", "seq", None),
        ),
        out_specs=(
            P("grp", "seq", None),
            P("grp", "seq", None),
            P(None, "grp", "seq"),
            P("grp", "seq"),
        ),
        check_vma=False,
    )
```

time: 251 us -> 58 us (0.23)
  waiting for transfers between devices: 159 us -> 0 us
  Pallas kernels: 0 us -> 50.6 us
  other arithmetic: 17.4 us -> 0 us
  matrix products: 17 us -> 0 us
  blocking collectives: 16.6 us -> 0 us
  between operations: 14.7 us -> 0.65 us
  starting transfers between devices: 12.2 us -> 0 us
  local copies, waits for them, and re-layouts: 13.8 us -> 6.45 us
    reduce_scatter x3 -> x0, waiting for transfers between devices: 88.7 us -> none  [the longest x1 37.5 us: body(): lax.psum_scatter(conv_part.astype(jnp.bfloat16), 'seq', scatter_dimension...]
    pallas_call x0 -> x1, Pallas kernels: none -> 50.6 us  [body(): pl.pallas_call(functools.partial(kernel, z, tuple(shapes)), out_shape=(ja...]
    unnamed x6 -> x0, waiting for transfers between devices: 48.6 us -> none
    all_gather x1 -> x0, waiting for transfers between devices: 21.9 us -> none  [body(): lax.all_gather(conv_weight, 'grp', axis=1, tiled=True)]
    dot_general x6 -> x0, matrix products: 17 us -> none  [the longest x1 5.47 us: body(): jnp.einsum('jrc,rd->jcd', shifted, hidden_grad, preferred_element_type=jn...]
    all_gather x1 -> x0, blocking collectives: 16.6 us -> none  [body(): lax.all_gather(proj_weight, 'grp', axis=0, tiled=True)]
    ppermute x6 -> x0, starting transfers between devices: 12 us -> none  [the longest x3 7.94 us: extended(): lax.ppermute(tail, axis, [(i, (i + 1) % count) for i in range(ends)])]
    unnamed x7 -> x0, other arithmetic: 9.39 us -> none
  transfers between devices with their start and end apart: 11 -> 0, of which waited for: 5 -> 0; matrix products, arithmetic and copies ran while one was open for 10% -> 0% of each run, Pallas kernels for 0% -> 0%
where the time goes in v1:
time: 58 us; the launch traced here: 57.7 us
  Pallas kernels  50.6 us (87%)
  local copies, waits for them, and re-layouts  6.45 us (11%)
  between operations  0.65 us (1%)
    pallas_call x1, Pallas kernels, body(): pl.pallas_call(functools.partial(kernel, z, tuple(shapes)), out_shape=(ja...  50.6 us
    unnamed x11, local copies, waits for them, and re-layouts  6.45 us

profile of v1, /device:TPU:0, one launch (start us, length us, event | category | flops | bytes accessed | tf_op | source)
XLA Modules:
  0.0 57.7 jit_solution(17017801158290197035)
XLA Ops:
  0.6 2.0 %copy.9 = bf16[1,512,448]{2,1,0:T(8,128)(2,1)} copy(bf16[1,512,448]{1,2,0:T(8,128)(2,1)} %param.9) | data formatting | bytes 917504 | tf_op args[4]
  2.6 50.6 %shard_map.84 = (bf16[512,448]{1,0:T(8,128)(2,1)}, bf16[1024,384]{1,0:T(8,128)(2,1)}, f32[5,48,96]{2,1,0:T(8,128)}, f32[56,96]{1,0:T(8,128)}) custom-call(bf16[1024,384]{1,0:T(8,128)(2,1)} %bitcast.7, s32[1,1024]{1,0:T(1,128)} %seg_ref.1, bf16[5,96,384]{2,1,0:T(8,128)(2,1)} %conv_ref.1, bf16[96,448]{1,0:T(8,128)(2,1)} %proj_ref.1, bf16[512,448]{1,0:T(8,128)(2,1)} %bitcast.6), custom_call_target="tpu_custom_call" | custom-call | tf_op jit(solution)/shard_map/pallas_call | solution.py:383
  53.2 0.0 copy-start
  53.2 2.1 %copy.10 = bf16[1,512,448]{1,2,0:T(8,128)(2,1)} copy(bf16[1,512,448]{2,1,0:T(8,128)(2,1)} %bitcast.9) | data formatting | bytes 917504
  55.3 0.0 copy-done
  55.3 0.0 copy-start.1
  55.3 0.9 %copy.14 = bf16[1,1024,384]{2,1,0:T(8,128)(2,1)} copy(bf16[1,1024,384]{2,1,0:T(8,128)(2,1)S(1)} %bitcast.8) | data formatting | bytes 1572864
  56.2 0.1 copy-done.1
  56.3 0.0 copy-start.2
  56.3 0.6 %copy.15 = f32[5,96,48]{1,2,0:T(8,128)} copy(f32[5,96,48]{1,2,0:T(8,128)S(1)} %bitcast.10) | data formatting | bytes 184320
  57.0 0.1 copy-done.2
  57.1 0.6 %copy.16 = f32[96,56]{0,1:T(8,128)} copy(f32[96,56]{0,1:T(8,128)S(1)} %bitcast.11) | data formatting | bytes 43008
Async XLA Ops:
  53.2 2.1 %copy-start = (bf16[1024,384]{1,0:T(8,128)(2,1)S(1)}, bf16[1024,384]{1,0:T(8,128)(2,1)}, u32[]{:S(2)}) copy-start(bf16[1024,384]{1,0:T(8,128)(2,1)} %get-tuple-element.9) | copy-start | bytes 2359300
  55.3 1.0 %copy-start.1 = (f32[5,48,96]{2,1,0:T(8,128)S(1)}, f32[5,48,96]{2,1,0:T(8,128)}, u32[]{:S(2)}) copy-start(f32[5,48,96]{2,1,0:T(8,128)} %get-tuple-element.10) | copy-start | bytes 276484
  56.3 0.7 %copy-start.2 = (f32[56,96]{1,0:T(8,128)S(1)}, f32[56,96]{1,0:T(8,128)}, u32[]{:S(2)}) copy-start(f32[56,96]{1,0:T(8,128)} %get-tuple-element.11) | copy-start | bytes 64516

commit v2 on v1

--- a/solution.py
+++ b/solution.py
@@ -43,11 +43,13 @@
         self.n_seq, self.n_grp = mesh.shape["seq"], mesh.shape["grp"]
         self.n_chip = self.n_seq // 2
         self.rows, self.c0 = x
-        self.half, self.c1 = cot
+        self.c1, self.half = cot
         self.cs = conv[1]
         self.gpt = -(-self.cs // 16)
         self.gpp = -(-TAPS * self.gpt // self.n_seq)
         self.ppp = -(-self.gpt // self.n_seq)
+        self.parts = 2 if self.gpp % 2 == 0 else 1
+        self.gpp //= self.parts
         self.dc, self.dp = self.c0 // self.n_seq, self.c1 // self.n_seq
         self.rc, self.rp = up16(self.dc), up16(self.dp)
         self.stage = BF16 if self.cs % 16 == 0 else F32
@@ -58,7 +60,6 @@
     V, S = pltpu.VMEM, pltpu.SemaphoreType.DMA
     shapes = dict(
         xh=V((2, EDGE, z.c0), BF16),
-        ch=V((2, EDGE, z.c1), BF16),
         sh=V((2, EDGE, 128), jnp.int32),
         seg=V((ext, 128), jnp.int32),
         act=V((ext, z.c0), F32),
@@ -67,19 +68,19 @@
         gradt=V((z.c0, z.rows), BF16),
         shifted=V((z.rows, TAPS * z.c0), BF16),
         pooled=V((z.half, z.c0), BF16),
-        wbuf=V((z.n_grp, z.n_chip, 2, 16 * z.gpp, z.c0), BF16),
+        wbuf=V((z.parts, z.n_grp, z.n_chip, 2, 16 * z.gpp, z.c0), BF16),
         pbuf=V((z.n_grp, z.n_chip, 2, 16 * z.ppp, z.c1), BF16),
         wf=V((TAPS * z.c0, z.c0), z.stage),
         wb=V((z.c0, TAPS * z.c0), z.stage),
         pf=V((z.c0, z.c1), z.stage),
         halo_s=S((6,)),
         halo_r=S((6,)),
-        gc_s=S((2, z.n_grp)),
-        gc_r=S((2, z.n_grp)),
-        gb_s=S((2, z.n_chip)),
-        gb_r=S((2, z.n_chip)),
-        ga_s=S((2,)),
-        ga_r=S((2,)),
+        gc_s=S((1 + z.parts, z.n_grp)),
+        gc_r=S((1 + z.parts, z.n_grp)),
+        gb_s=S((1 + z.parts, z.n_chip)),
+        gb_r=S((1 + z.parts, z.n_chip)),
+        ga_s=S((1 + z.parts,)),
+        ga_r=S((1 + z.parts,)),
         ra_s=S((TAPS + 1,)),
         ra_r=S((TAPS + 1,)),
         rb_s=S((TAPS + 1, z.n_chip)),
@@ -145,11 +146,15 @@
     for to in peers:
         pl.semaphore_signal(barrier, inc=1, device_id=to, device_id_type=pl.DeviceIdType.MESH)
 
+    def tap_place(q):
+        part, q = divmod(q, z.gpp * z.n_seq)
+        return part, q // z.gpp, (q % z.gpp) * 16
+
     for q in range(TAPS * z.gpt):
         j, r = q // z.gpt, (q % z.gpt) * 16
         h = min(16, z.cs - r)
-        piece, o = q // z.gpp, (q % z.gpp) * 16
-        m["wbuf"][0, piece // 2, piece % 2, o : o + h, :] = conv_ref[j, r : r + h, :]
+        part, piece, o = tap_place(q)
+        m["wbuf"][part, 0, piece // 2, piece % 2, o : o + h, :] = conv_ref[j, r : r + h, :]
     for q in range(z.gpt):
         r = q * 16
         h = min(16, z.cs - r)
@@ -178,17 +183,20 @@
     go(pc := gather_c(0, m["pbuf"]))
     halos = []
     ends = (pl.ds(0, EDGE), pl.ds(z.rows - EDGE, EDGE))
-    cot_ends = (pl.ds(0, EDGE), pl.ds(z.half - EDGE, EDGE))
     seg_ends = (pl.ds(EDGE, EDGE), pl.ds(z.rows, EDGE))
     for i, (src, dst, cuts) in enumerate(
-        ((x_ref, m["xh"], ends), (cot_ref, m["ch"], cot_ends), (m["seg"], m["sh"], seg_ends))
+        ((x_ref, m["xh"], ends), (m["seg"], m["sh"], seg_ends))
     ):
         for side, to in ((1, left), (0, right)):
             halos.append(remote(
                 src.at[cuts[1 - side]], dst.at[side], m["halo_s"].at[2 * i + side], m["halo_r"].at[2 * i + side], at(to, g)
             ))
     go(halos)
-    go(wc := gather_c(1, m["wbuf"]))
+    taps_buf = [m["wbuf"].at[i] for i in range(z.parts)]
+    wc = [gather_c(1 + i, buf) for i, buf in enumerate(taps_buf)]
+    wb, wa = [None] * z.parts, [None] * z.parts
+    for copies in wc:
+        go(copies)
 
     def act_rows(first, count):
         def step(t, _):
@@ -199,14 +207,21 @@
             m["slope"][pl.ds(b, 32), :] = cdf + r * (jnp.exp(-0.5 * r * r) * (1.0 / math.sqrt(2.0 * math.pi)))
             return 0
 
-        lax.fori_loop(first // 32, (first + count) // 32, step, 0)
-
-    act_rows(0, z.rows // 2)
+        lax.fori_loop(first // 32, (first + count) // 32, step, 0, unroll=4)
+
+    quarter = z.rows // 4
+    act_rows(0, quarter)
     landed(pc)
     go(pb := gather_b(0, m["pbuf"]))
-    act_rows(z.rows // 2, z.rows // 2)
-    landed(wc)
-    go(wb := gather_b(1, m["wbuf"]))
+    act_rows(quarter, quarter)
+    act_rows(2 * quarter, quarter)
+    landed(pb)
+    go(pa := gather_a(0, m["pbuf"]))
+    landed(wc[0])
+    go_b = gather_b(1, taps_buf[0])
+    go(go_b)
+    wb[0] = go_b
+    act_rows(3 * quarter, quarter)
 
     landed(halos)
     for side, where in ((0, 0), (1, EDGE + z.rows)):
@@ -214,9 +229,6 @@
         m["act"][where : where + EDGE, :] = (r * gate(r)).astype(BF16).astype(F32)
         outside = (s == 0) if side == 0 else (s == z.n_seq - 1)
         m["seg"][where : where + EDGE, :] = jnp.where(outside, -1, m["sh"][side])
-
-    landed(pb)
-    go(pa := gather_a(0, m["pbuf"]))
 
     def spread(src):
         def step(t, _):
@@ -231,8 +243,12 @@
                     m["shifted"][pl.ds(b, 64), j * z.c0 + o : j * z.c0 + o + 128] = cut
             return 0
 
-        lax.fori_loop(0, z.rows // 64, step, 0)
-
+        lax.fori_loop(0, z.rows // 64, step, 0, unroll=2)
+
+    for i in range(1, z.parts):
+        landed(wc[i])
+        wb[i] = gather_b(1 + i, taps_buf[i])
+        go(wb[i])
     spread(m["act"])
 
     landed(pa)
@@ -246,19 +262,25 @@
             m["pf"][pl.ds(pl.multiple_of(base + r, math.gcd(z.cs, 16)), h), :] = rows
     proj = m["pf"][...].astype(BF16)
 
-    pool_grad = (dot(cot_ref[...], proj, NT) * 0.5).astype(BF16)
-    double = pick(256, 128, 0, 2).astype(BF16)
+    pool_grad = (dot(proj, cot_ref[...]) * 0.5).astype(BF16)
+    double = pick(256, 128, 0, 2)
+    double_t = double.T.astype(BF16)
+    double = double.astype(BF16)
     for t in range(z.half // 128):
-        hg = dot(double, pool_grad[t * 128 : t * 128 + 128])
-        m["grad"][EDGE + t * 256 : EDGE + t * 256 + 256, :] = hg
-        m["gradt"][:, t * 256 : t * 256 + 256] = hg.T.astype(BF16)
-    for side, where in ((0, 0), (1, EDGE + z.rows)):
-        pg = (dot(m["ch"][side], proj, NT) * 0.5).astype(BF16)
-        chosen = pick(EDGE, EDGE, EDGE // 2 if side == 0 else 0, 2).astype(BF16)
-        m["grad"][where : where + EDGE, :] = dot(chosen, pg)
-
-    landed(wb)
-    go(wa := gather_a(1, m["wbuf"]))
+        block = pool_grad[:, t * 128 : t * 128 + 128]
+        m["grad"][EDGE + t * 256 : EDGE + t * 256 + 256, :] = dot(double, block, NT)
+        m["gradt"][:, t * 256 : t * 256 + 256] = dot(block, double_t).astype(BF16)
+    edges = []
+    for i, (src, dst, to) in enumerate(((EDGE, EDGE + z.rows, left), (EDGE + z.rows - 8, EDGE - 8, right))):
+        edges.append(remote(
+            m["grad"].at[pl.ds(src, 8)], m["grad"].at[pl.ds(dst, 8)], m["halo_s"].at[4 + i], m["halo_r"].at[4 + i], at(to, g)
+        ))
+    go(edges)
+    proj_t = proj.T
+
+    landed(wb[0])
+    wa[0] = gather_a(1, taps_buf[0])
+    go(wa[0])
 
     def unit(u):
         return ("c", u, z.dc) if u < TAPS else ("p", 0, z.dp)
@@ -320,24 +342,28 @@
 
     for j in range(TAPS):
         reduce_a(j, dot(m["gradt"][...], m["shifted"][:, j * z.c0 : j * z.c0 + z.c0]))
-        if j >= 1:
-            reduce_b(j - 1)
-        if j >= 3:
-            reduce_c(j - 3)
-
-    landed(wa)
+        if j >= 2:
+            reduce_b(j - 2)
+        if j == 2:
+            for i in range(1, z.parts):
+                landed(wb[i])
+                wa[i] = gather_a(1 + i, taps_buf[i])
+                go(wa[i])
+
+    for copies in wa:
+        landed(copies)
     for k in range(z.n_grp):
         base = lax.rem(g + z.n_grp - k, z.n_grp) * z.cs
         for q in range(TAPS * z.gpt):
             j, r = q // z.gpt, (q % z.gpt) * 16
             h = min(16, z.cs - r)
-            piece, o = q // z.gpp, (q % z.gpp) * 16
-            rows = m["wbuf"][k, piece // 2, piece % 2, o : o + h, :].astype(z.stage)
+            part, piece, o = tap_place(q)
+            rows = m["wbuf"][part, k, piece // 2, piece % 2, o : o + h, :].astype(z.stage)
             place = pl.multiple_of(base + r, math.gcd(z.cs, 16))
             m["wf"][pl.ds(j * z.c0 + place, h), :] = rows
             m["wb"][pl.ds(place, h), (TAPS - 1 - j) * z.c0 : (TAPS - j) * z.c0] = rows
-    reduce_b(TAPS - 1)
-    reduce_c(2)
+    reduce_b(3)
+    reduce_b(4)
 
     halve = (pick(256, 128, 0, 2).T * 0.5).astype(BF16)
     for t in range(z.rows // 256):
@@ -345,20 +371,23 @@
         conv = dot(m["shifted"][a : a + 256, :], m["wf"][...].astype(BF16))
         hidden = (x_ref[a : a + 256, :].astype(F32) + conv).astype(BF16)
         m["pooled"][a // 2 : a // 2 + 128, :] = dot(halve, hidden).astype(BF16)
-    reduce_c(3)
     pooled = m["pooled"][...]
-    reduce_a(TAPS, dot(cot_ref[...].T, pooled))
-    po_ref[...] = dot(pooled, proj).astype(BF16)
-    reduce_c(4)
-
+    reduce_a(TAPS, dot(cot_ref[...], pooled))
+    reduce_c(0)
+    reduce_c(1)
+    po_ref[...] = dot(proj_t, pooled, NT).astype(BF16)
+
+    landed(edges)
     spread(m["grad"])
     reduce_b(TAPS)
+    reduce_c(2)
     for t in range(z.rows // 256):
         a = t * 256
         act_grad = dot(m["shifted"][a : a + 256, :], m["wb"][...].astype(BF16), NT)
         m["act"][a : a + 256, :] = act_grad * m["slope"][a : a + 256, :]
         if t == 1:
-            reduce_c(TAPS)
+            reduce_c(3)
+    reduce_c(4)
 
     def last(t, _):
         b = pl.multiple_of(t * 32, 32)
@@ -368,7 +397,9 @@
         ig_ref[pl.ds(b, 32), :] = (m["grad"][pl.ds(EDGE + b, 32), :] + centred * inverse).astype(BF16)
         return 0
 
-    lax.fori_loop(0, z.rows // 32, last, 0)
+    lax.fori_loop(0, z.rows // 64, last, 0, unroll=4)
+    reduce_c(TAPS)
+    lax.fori_loop(z.rows // 64, z.rows // 32, last, 0, unroll=4)
     for u in range(TAPS + 1):
         reduce_end(u)
     for c in sent:
@@ -376,14 +407,14 @@
 
 
 def body(mesh, inputs, segment, conv_weight, proj_weight, cotangent):
-    z = Sizes(mesh, inputs.shape[1:], conv_weight.shape, proj_weight.shape, cotangent.shape[1:])
+    z = Sizes(mesh, inputs.shape[1:], conv_weight.shape, proj_weight.shape, cotangent.shape[:0:-1])
     shapes = scratch(z)
     vmem = pl.BlockSpec(memory_space=pltpu.VMEM)
     lanes = z.c0 // z.n_grp
     po, ig, cg, pg = pl.pallas_call(
         functools.partial(kernel, z, tuple(shapes)),
         out_shape=(
-            jax.ShapeDtypeStruct((z.half, z.c1), BF16),
+            jax.ShapeDtypeStruct((z.c1, z.half), BF16),
             jax.ShapeDtypeStruct((z.rows, z.c0), BF16),
             jax.ShapeDtypeStruct((TAPS, z.dc, lanes), F32),
             jax.ShapeDtypeStruct((z.dp, lanes), F32),
@@ -394,8 +425,8 @@
         compiler_params=pltpu.CompilerParams(
             collective_id=0, has_side_effects=True, vmem_limit_bytes=56 * 1024 * 1024
         ),
-    )(inputs[0], segment, conv_weight, proj_weight, cotangent[0])
-    return po[None], ig[None], jnp.swapaxes(cg, 1, 2), pg.T
+    )(inputs[0], segment, conv_weight, proj_weight, cotangent[0].T)
+    return po.T[None], ig[None], jnp.swapaxes(cg, 1, 2), pg.T
 
 
 def solution(mesh):

time: 58 us -> 47.8 us (0.82)
  Pallas kernels: 50.6 us -> 42.7 us
  local copies, waits for them, and re-layouts: 6.45 us -> 4.24 us
    pallas_call x1, Pallas kernels: 50.6 us -> 42.7 us  [body(): pl.pallas_call(functools.partial(kernel, z, tuple(shapes)), out_shape=(ja...]
    unnamed x11 -> x10, local copies, waits for them, and re-layouts: 6.45 us -> 4.24 us
where the time goes in v2:
time: 47.8 us; the launch traced here: 47.5 us
  Pallas kernels  42.7 us (89%)
  local copies, waits for them, and re-layouts  4.24 us (9%)
  between operations  0.65 us (1%)
    pallas_call x1, Pallas kernels, body(): pl.pallas_call(functools.partial(kernel, z, tuple(shapes)), out_shape=(ja...  42.7 us
    unnamed x10, local copies, waits for them, and re-layouts  4.24 us

profile of v2, /device:TPU:0, one launch (start us, length us, event | category | flops | bytes accessed | tf_op | source)
XLA Modules:
  0.0 47.5 jit_solution(15391476054681421730)
XLA Ops:
  0.6 42.7 %shard_map.84 = (bf16[448,512]{1,0:T(8,128)(2,1)}, bf16[1024,384]{1,0:T(8,128)(2,1)}, f32[5,48,96]{2,1,0:T(8,128)}, f32[56,96]{1,0:T(8,128)}) custom-call(bf16[1024,384]{1,0:T(8,128)(2,1)} %bitcast.11, s32[1,1024]{1,0:T(1,128)} %seg_ref.1, bf16[5,96,384]{2,1,0:T(8,128)(2,1)} %conv_ref.1, bf16[96,448]{1,0:T(8,128)(2,1)} %proj_ref.1, bf16[448,512]{1,0:T(8,128)(2,1)} %bitcast.13), custom_call_target="tpu_custom_call" | custom-call | tf_op jit(solution)/shard_map/pallas_call | solution.py:414
  43.3 0.0 copy-start
  43.3 1.9 %copy.13 = bf16[1,512,448]{1,2,0:T(8,128)(2,1)} copy(bf16[1,512,448]{1,2,0:T(8,128)(2,1)} %bitcast.12) | data formatting | bytes 917504
  45.2 0.0 copy-done
  45.2 0.0 copy-start.1
  45.2 0.9 %copy.14 = bf16[1,1024,384]{2,1,0:T(8,128)(2,1)} copy(bf16[1,1024,384]{2,1,0:T(8,128)(2,1)S(1)} %bitcast.10) | data formatting | bytes 1572864
  46.1 0.1 copy-done.1
  46.2 0.0 copy-start.2
  46.2 0.6 %copy.15 = f32[5,96,48]{1,2,0:T(8,128)} copy(f32[5,96,48]{1,2,0:T(8,128)S(1)} %bitcast.14) | data formatting | bytes 184320
  46.8 0.1 copy-done.2
  46.9 0.6 %copy.16 = f32[96,56]{0,1:T(8,128)} copy(f32[96,56]{0,1:T(8,128)S(1)} %bitcast.15) | data formatting | bytes 43008
Async XLA Ops:
  43.3 1.9 %copy-start = (bf16[1024,384]{1,0:T(8,128)(2,1)S(1)}, bf16[1024,384]{1,0:T(8,128)(2,1)}, u32[]{:S(2)}) copy-start(bf16[1024,384]{1,0:T(8,128)(2,1)} %get-tuple-element.9) | copy-start | bytes 2359300
  45.2 1.0 %copy-start.1 = (f32[5,48,96]{2,1,0:T(8,128)S(1)}, f32[5,48,96]{2,1,0:T(8,128)}, u32[]{:S(2)}) copy-start(f32[5,48,96]{2,1,0:T(8,128)} %get-tuple-element.10) | copy-start | bytes 276484
  46.2 0.7 %copy-start.2 = (f32[56,96]{1,0:T(8,128)S(1)}, f32[56,96]{1,0:T(8,128)}, u32[]{:S(2)}) copy-start(f32[56,96]{1,0:T(8,128)} %get-tuple-element.11) | copy-start | bytes 64516

commit v3 on v2

--- a/solution.py
+++ b/solution.py
@@ -48,7 +48,7 @@
         self.gpt = -(-self.cs // 16)
         self.gpp = -(-TAPS * self.gpt // self.n_seq)
         self.ppp = -(-self.gpt // self.n_seq)
-        self.parts = 2 if self.gpp % 2 == 0 else 1
+        self.parts = self.gpp if self.gpp <= 4 else 1
         self.gpp //= self.parts
         self.dc, self.dp = self.c0 // self.n_seq, self.c1 // self.n_seq
         self.rc, self.rp = up16(self.dc), up16(self.dp)
@@ -209,19 +209,24 @@
 
         lax.fori_loop(first // 32, (first + count) // 32, step, 0, unroll=4)
 
-    quarter = z.rows // 4
-    act_rows(0, quarter)
+    def forward_b(i):
+        if i < z.parts:
+            landed(wc[i])
+            wb[i] = gather_b(1 + i, taps_buf[i])
+            go(wb[i])
+
+    def forward_a(i):
+        if i < z.parts:
+            landed(wb[i])
+            wa[i] = gather_a(1 + i, taps_buf[i])
+            go(wa[i])
+
+    half = z.rows // 2
+    act_rows(0, half)
     landed(pc)
     go(pb := gather_b(0, m["pbuf"]))
-    act_rows(quarter, quarter)
-    act_rows(2 * quarter, quarter)
-    landed(pb)
-    go(pa := gather_a(0, m["pbuf"]))
-    landed(wc[0])
-    go_b = gather_b(1, taps_buf[0])
-    go(go_b)
-    wb[0] = go_b
-    act_rows(3 * quarter, quarter)
+    act_rows(half, half)
+    forward_b(0)
 
     landed(halos)
     for side, where in ((0, 0), (1, EDGE + z.rows)):
@@ -230,7 +235,7 @@
         outside = (s == 0) if side == 0 else (s == z.n_seq - 1)
         m["seg"][where : where + EDGE, :] = jnp.where(outside, -1, m["sh"][side])
 
-    def spread(src):
+    def spread(src, part):
         def step(t, _):
             b = pl.multiple_of(t * 64, 64)
             seg = m["seg"][pl.ds(b, 64 + 2 * EDGE), :]
@@ -243,13 +248,15 @@
                     m["shifted"][pl.ds(b, 64), j * z.c0 + o : j * z.c0 + o + 128] = cut
             return 0
 
-        lax.fori_loop(0, z.rows // 64, step, 0, unroll=2)
-
-    for i in range(1, z.parts):
-        landed(wc[i])
-        wb[i] = gather_b(1 + i, taps_buf[i])
-        go(wb[i])
-    spread(m["act"])
+        n = z.rows // 128
+        lax.fori_loop(part * n, part * n + n, step, 0, unroll=2)
+
+    spread(m["act"], 0)
+    forward_b(1)
+    landed(pb)
+    go(pa := gather_a(0, m["pbuf"]))
+    spread(m["act"], 1)
+    forward_b(2)
 
     landed(pa)
     for k in range(z.n_grp):
@@ -278,9 +285,8 @@
     go(edges)
     proj_t = proj.T
 
-    landed(wb[0])
-    wa[0] = gather_a(1, taps_buf[0])
-    go(wa[0])
+    forward_b(3)
+    forward_a(0)
 
     def unit(u):
         return ("c", u, z.dc) if u < TAPS else ("p", 0, z.dp)
@@ -342,28 +348,38 @@
 
     for j in range(TAPS):
         reduce_a(j, dot(m["gradt"][...], m["shifted"][:, j * z.c0 : j * z.c0 + z.c0]))
-        if j >= 2:
-            reduce_b(j - 2)
-        if j == 2:
-            for i in range(1, z.parts):
-                landed(wb[i])
-                wa[i] = gather_a(1 + i, taps_buf[i])
-                go(wa[i])
-
-    for copies in wa:
-        landed(copies)
-    for k in range(z.n_grp):
-        base = lax.rem(g + z.n_grp - k, z.n_grp) * z.cs
-        for q in range(TAPS * z.gpt):
-            j, r = q // z.gpt, (q % z.gpt) * 16
-            h = min(16, z.cs - r)
-            part, piece, o = tap_place(q)
-            rows = m["wbuf"][part, k, piece // 2, piece % 2, o : o + h, :].astype(z.stage)
-            place = pl.multiple_of(base + r, math.gcd(z.cs, 16))
-            m["wf"][pl.ds(j * z.c0 + place, h), :] = rows
-            m["wb"][pl.ds(place, h), (TAPS - 1 - j) * z.c0 : (TAPS - j) * z.c0] = rows
+        if j == 1:
+            forward_a(1)
+        if j == 3:
+            forward_a(2)
+
+    def assemble(i):
+        if i >= z.parts:
+            return
+        landed(wa[i])
+        for k in range(z.n_grp):
+            base = lax.rem(g + z.n_grp - k, z.n_grp) * z.cs
+            for q in range(TAPS * z.gpt):
+                part, piece, o = tap_place(q)
+                if part != i:
+                    continue
+                j, r = q // z.gpt, (q % z.gpt) * 16
+                h = min(16, z.cs - r)
+                rows = m["wbuf"][part, k, piece // 2, piece % 2, o : o + h, :].astype(z.stage)
+                place = pl.multiple_of(base + r, math.gcd(z.cs, 16))
+                m["wf"][pl.ds(j * z.c0 + place, h), :] = rows
+                m["wb"][pl.ds(place, h), (TAPS - 1 - j) * z.c0 : (TAPS - j) * z.c0] = rows
+
+    reduce_b(0)
+    assemble(0)
+    assemble(1)
+    reduce_b(1)
+    forward_a(3)
+    reduce_b(2)
+    assemble(2)
     reduce_b(3)
     reduce_b(4)
+    assemble(3)
 
     halve = (pick(256, 128, 0, 2).T * 0.5).astype(BF16)
     for t in range(z.rows // 256):
@@ -378,16 +394,10 @@
     po_ref[...] = dot(proj_t, pooled, NT).astype(BF16)
 
     landed(edges)
-    spread(m["grad"])
+    spread(m["grad"], 0)
     reduce_b(TAPS)
     reduce_c(2)
-    for t in range(z.rows // 256):
-        a = t * 256
-        act_grad = dot(m["shifted"][a : a + 256, :], m["wb"][...].astype(BF16), NT)
-        m["act"][a : a + 256, :] = act_grad * m["slope"][a : a + 256, :]
-        if t == 1:
-            reduce_c(3)
-    reduce_c(4)
+    spread(m["grad"], 1)
 
     def last(t, _):
         b = pl.multiple_of(t * 32, 32)
@@ -397,13 +407,34 @@
         ig_ref[pl.ds(b, 32), :] = (m["grad"][pl.ds(EDGE + b, 32), :] + centred * inverse).astype(BF16)
         return 0
 
-    lax.fori_loop(0, z.rows // 64, last, 0, unroll=4)
-    reduce_c(TAPS)
-    lax.fori_loop(z.rows // 64, z.rows // 32, last, 0, unroll=4)
+    for t in range(z.rows // 256):
+        a = t * 256
+        act_grad = dot(m["shifted"][a : a + 256, :], m["wb"][...].astype(BF16), NT)
+        m["act"][a : a + 256, :] = act_grad * m["slope"][a : a + 256, :]
+        if t == 0:
+            reduce_c(3)
+        if t == 1:
+            reduce_c(4)
+        if t == 2:
+            reduce_c(TAPS)
+        lax.fori_loop(a // 32, a // 32 + 8, last, 0, unroll=4)
     for u in range(TAPS + 1):
         reduce_end(u)
     for c in sent:
         c.wait_send()
+
+
+def finish(*refs):
+    ins, outs, held, came, left = refs[:4], refs[4:8], refs[8:12], refs[12], refs[13]
+    first = [pltpu.make_async_copy(a, b, came.at[i]) for i, (a, b) in enumerate(zip(ins, held))]
+    then = [pltpu.make_async_copy(a, b, left.at[i]) for i, (a, b) in enumerate(zip(held, outs))]
+    for c in first:
+        c.start()
+    for c, d in zip(first, then):
+        c.wait()
+        d.start()
+    for d in then:
+        d.wait()
 
 
 def body(mesh, inputs, segment, conv_weight, proj_weight, cotangent):
@@ -426,6 +457,15 @@
             collective_id=0, has_side_effects=True, vmem_limit_bytes=56 * 1024 * 1024
         ),
     )(inputs[0], segment, conv_weight, proj_weight, cotangent[0].T)
+    outs = (po, ig, cg, pg)
+    po, ig, cg, pg = pl.pallas_call(
+        finish,
+        out_shape=tuple(jax.ShapeDtypeStruct(o.shape, o.dtype) for o in outs),
+        in_specs=[pl.BlockSpec(memory_space=pl.ANY)] * 4,
+        out_specs=[pl.BlockSpec(memory_space=pl.ANY)] * 4,
+        scratch_shapes=[pltpu.VMEM(o.shape, o.dtype) for o in outs] + [pltpu.SemaphoreType.DMA((4,))] * 2,
+        compiler_params=pltpu.CompilerParams(vmem_limit_bytes=56 * 1024 * 1024),
+    )(*outs)
     return po.T[None], ig[None], jnp.swapaxes(cg, 1, 2), pg.T
 
 

time: 47.8 us -> 44.6 us (0.933)
  local copies, waits for them, and re-layouts: 4.24 us -> 0 us
  Pallas kernels: 42.7 us -> 43.8 us
    unnamed x10 -> x0, local copies, waits for them, and re-layouts: 4.24 us -> none
    pallas_call x0 -> x1, Pallas kernels: none -> 2.25 us  [body(): pl.pallas_call(finish, out_shape=tuple((jax.ShapeDtypeStruct(o.shape, o.d...]
    pallas_call x1, Pallas kernels: 42.7 us -> 41.5 us  [body(): pl.pallas_call(functools.partial(kernel, z, tuple(shapes)), out_shape=(ja...]
where the time goes in v3:
time: 44.6 us; the launch traced here: 44.4 us
  Pallas kernels  43.8 us (98%)
  between operations  0.64 us (1%)
    pallas_call x1, Pallas kernels, body(): pl.pallas_call(functools.partial(kernel, z, tuple(shapes)), out_shape=(ja...  41.5 us
    pallas_call x1, Pallas kernels, body(): pl.pallas_call(finish, out_shape=tuple((jax.ShapeDtypeStruct(o.shape, o.d...  2.25 us

profile of v3, /device:TPU:0, one launch (start us, length us, event | category | flops | bytes accessed | tf_op | source)
XLA Modules:
  0.0 44.4 jit_solution(18166759463537555526)
XLA Ops:
  0.6 41.5 %shard_map.84 = (bf16[448,512]{1,0:T(8,128)(2,1)}, bf16[1024,384]{1,0:T(8,128)(2,1)}, f32[5,48,96]{2,1,0:T(8,128)}, f32[56,96]{1,0:T(8,128)}) custom-call(bf16[1024,384]{1,0:T(8,128)(2,1)} %bitcast.10, s32[1,1024]{1,0:T(1,128)} %seg_ref.1, bf16[5,96,384]{2,1,0:T(8,128)(2,1)} %conv_ref.1, bf16[96,448]{1,0:T(8,128)(2,1)} %proj_ref.1, bf16[448,512]{1,0:T(8,128)(2,1)} %bitcast.11), custom_call_target="tpu_custom_call" | custom-call | tf_op jit(solution)/shard_map/pallas_call | solution.py:445
  42.2 2.3 %shard_map.85 = (bf16[448,512]{1,0:T(8,128)(2,1)}, bf16[1024,384]{1,0:T(8,128)(2,1)}, f32[5,48,96]{2,1,0:T(8,128)}, f32[56,96]{1,0:T(8,128)}) custom-call(bf16[448,512]{1,0:T(8,128)(2,1)} %get-tuple-element.12.refs_0_, bf16[1024,384]{1,0:T(8,128)(2,1)} %get-tuple-element.13.refs_1_, f32[5,48,96]{2,1,0:T(8,128)} %get-tuple-element.14.refs_2_, ...), custom_call_target="tpu_custom_call" | custom-call | tf_op jit(solution)/shard_map/pallas_call | solution.py:461

commit v4 on v3

--- a/solution.py
+++ b/solution.py
@@ -181,6 +181,12 @@
         return [remote(part, part, m["ga_s"].at[i], m["ga_r"].at[i], at(sibling, g))]
 
     go(pc := gather_c(0, m["pbuf"]))
+    taps_buf = [m["wbuf"].at[i] for i in range(z.parts)]
+    wc = [gather_c(1 + i, buf) for i, buf in enumerate(taps_buf)]
+    wb, wa = [None] * z.parts, [None] * z.parts
+    for copies in wc:
+        go(copies)
+
     halos = []
     ends = (pl.ds(0, EDGE), pl.ds(z.rows - EDGE, EDGE))
     seg_ends = (pl.ds(EDGE, EDGE), pl.ds(z.rows, EDGE))
@@ -192,12 +198,6 @@
                 src.at[cuts[1 - side]], dst.at[side], m["halo_s"].at[2 * i + side], m["halo_r"].at[2 * i + side], at(to, g)
             ))
     go(halos)
-    taps_buf = [m["wbuf"].at[i] for i in range(z.parts)]
-    wc = [gather_c(1 + i, buf) for i, buf in enumerate(taps_buf)]
-    wb, wa = [None] * z.parts, [None] * z.parts
-    for copies in wc:
-        go(copies)
-
     def act_rows(first, count):
         def step(t, _):
             b = pl.multiple_of(t * 32, 32)
@@ -249,7 +249,7 @@
             return 0
 
         n = z.rows // 128
-        lax.fori_loop(part * n, part * n + n, step, 0, unroll=2)
+        lax.fori_loop(part * n, part * n + n, step, 0, unroll=4)
 
     spread(m["act"], 0)
     forward_b(1)
@@ -389,13 +389,13 @@
         m["pooled"][a // 2 : a // 2 + 128, :] = dot(halve, hidden).astype(BF16)
     pooled = m["pooled"][...]
     reduce_a(TAPS, dot(cot_ref[...], pooled))
+    po_ref[...] = dot(proj_t, pooled, NT).astype(BF16)
+
+    landed(edges)
+    reduce_b(TAPS)
     reduce_c(0)
+    spread(m["grad"], 0)
     reduce_c(1)
-    po_ref[...] = dot(proj_t, pooled, NT).astype(BF16)
-
-    landed(edges)
-    spread(m["grad"], 0)
-    reduce_b(TAPS)
     reduce_c(2)
     spread(m["grad"], 1)
 
@@ -417,7 +417,7 @@
             reduce_c(4)
         if t == 2:
             reduce_c(TAPS)
-        lax.fori_loop(a // 32, a // 32 + 8, last, 0, unroll=4)
+        lax.fori_loop(a // 32, a // 32 + 8, last, 0, unroll=8)
     for u in range(TAPS + 1):
         reduce_end(u)
     for c in sent:

time: 44.6 us -> 44.2 us (level)
  Pallas kernels: 43.8 us -> 43.2 us
    pallas_call x1, Pallas kernels: 41.5 us -> 41 us  [body(): pl.pallas_call(functools.partial(kernel, z, tuple(shapes)), out_shape=(ja...]
where the time goes in v4:
time: 44.2 us; the launch traced here: 44 us
  Pallas kernels  43.2 us (98%)
  between operations  0.8 us (2%)
    pallas_call x1, Pallas kernels, body(): pl.pallas_call(functools.partial(kernel, z, tuple(shapes)), out_shape=(ja...  41 us
    pallas_call x1, Pallas kernels, body(): pl.pallas_call(finish, out_shape=tuple((jax.ShapeDtypeStruct(o.shape, o.d...  2.25 us

profile of v4, /device:TPU:0, one launch (start us, length us, event | category | flops | bytes accessed | tf_op | source)
XLA Modules:
  0.0 44.0 jit_solution(17498111592424796767)
XLA Ops:
  0.6 41.0 %shard_map.84 = (bf16[448,512]{1,0:T(8,128)(2,1)}, bf16[1024,384]{1,0:T(8,128)(2,1)}, f32[5,48,96]{2,1,0:T(8,128)}, f32[56,96]{1,0:T(8,128)}) custom-call(bf16[1024,384]{1,0:T(8,128)(2,1)} %bitcast.10, s32[1,1024]{1,0:T(1,128)} %seg_ref.1, bf16[5,96,384]{2,1,0:T(8,128)(2,1)} %conv_ref.1, bf16[96,448]{1,0:T(8,128)(2,1)} %proj_ref.1, bf16[448,512]{1,0:T(8,128)(2,1)} %bitcast.11), custom_call_target="tpu_custom_call" | custom-call | tf_op jit(solution)/shard_map/pallas_call | solution.py:445
  41.6 2.3 %shard_map.85 = (bf16[448,512]{1,0:T(8,128)(2,1)}, bf16[1024,384]{1,0:T(8,128)(2,1)}, f32[5,48,96]{2,1,0:T(8,128)}, f32[56,96]{1,0:T(8,128)}) custom-call(bf16[448,512]{1,0:T(8,128)(2,1)} %get-tuple-element.12.refs_0_, bf16[1024,384]{1,0:T(8,128)(2,1)} %get-tuple-element.13.refs_1_, f32[5,48,96]{2,1,0:T(8,128)} %get-tuple-element.14.refs_2_, ...), custom_call_target="tpu_custom_call" | custom-call | tf_op jit(solution)/shard_map/pallas_call | solution.py:461
